TPU v7x, 32 devices: a whole 2x2x4 slice. The times are simulated.
32 devices in a mesh: grp: 4 (over x, core), row: 8 (over z, y).
Axes of the slice: x: 2, y: 2, z: 4, core: 2. Of those that a mesh axis runs over, the one named last changes fastest.
Arguments:
- inputs: bfloat16 [16384, 2048], P(('grp', 'row')), may hold values from -6 to 6
- norm_gain: float32 [2048], replicated, may hold values from 0.25 to 1.75
- w_hidden: bfloat16 [2048, 2048], replicated, may hold values from -0.125 to 0.125
- w_proj: bfloat16 [2048, 256], replicated, may hold values from -0.125 to 0.125
- observed: float32 [16384], P(('grp', 'row')), may hold values from -6 to 6
- evolved: float32 [16384], P(('grp', 'row')), may hold values from -6 to 6
- station_ids: int32 [16384], P(('grp', 'row')), may hold values from 0 to 511
- station_gain: float32 [512], replicated, may hold values from 0.3 to 3
- station_offset: float32 [512], replicated, may hold values from -4 to 4
Outputs:
- grad_hidden: float32 [2048, 2048], P(('grp', 'row'))
- grad_proj: float32 [2048, 256], P(('grp', 'row'))
Inputs may be any that keep to these rules, and one draw needn't show every extreme that they name: `station_ids`: a station number for every row.
All inputs are finite; a program needn't handle non-finite values.
Results may differ from a plain program's by a relative error of at most 0.0068.
Values sent between devices are 32-bit elements; how exact they have to be, the bound alone decides.
A program may use at most 128 MiB of HBM per device.

v0:
```python
import jax
import jax.numpy as jnp
from jax import lax
from jax.sharding import PartitionSpec as P


def forward(rows_in, norm_gain, w_hidden, w_proj):
    values = rows_in.astype(jnp.float32)
    mean_square = jnp.mean(values * values, axis=1, keepdims=True)
    normed = (values * lax.rsqrt(mean_square + 1e-06) * norm_gain).astype(jnp.bfloat16)
    pre = jnp.dot(normed, w_hidden, preferred_element_type=jnp.float32)
    hidden = (values + jax.nn.silu(pre)).astype(jnp.bfloat16)
    features = jnp.dot(hidden, w_proj, preferred_element_type=jnp.float32)
    return (normed, pre, hidden, features)


def make_target(observed, evolved, station_ids, station_gain, station_offset):
    onehot = (
        station_ids[:, None] == jnp.arange(station_gain.shape[0], dtype=jnp.int32)[None, :]
    ).astype(jnp.float32)
    gain_rows = jnp.dot(onehot, station_gain, precision=lax.Precision.HIGHEST)
    offset_rows = jnp.dot(onehot, station_offset, precision=lax.Precision.HIGHEST)
    return observed - gain_rows * evolved - offset_rows


def contract_rows(left, right, precision=None):
    return lax.dot_general(
        left,
        right,
        (((0,), (0,)), ((), ())),
        precision=precision,
        preferred_element_type=jnp.float32,
    )


def body(
    inputs,
    norm_gain,
    w_hidden,
    w_proj,
    observed,
    evolved,
    station_ids,
    station_gain,
    station_offset,
):
    width = inputs.shape[1]
    feat_width = w_proj.shape[1]
    normed, pre, hidden, features = forward(inputs, norm_gain, w_hidden, w_proj)
    target = make_target(observed, evolved, station_ids, station_gain, station_offset)
    gram_part = contract_rows(features, features, lax.Precision.HIGHEST)
    moment_part = contract_rows(features, target[:, None], lax.Precision.HIGHEST)[:, 0]
    gram, moment = lax.psum((gram_part, moment_part), ("grp", "row"))
    gram = gram + jnp.eye(feat_width, dtype=jnp.float32)
    factor = jnp.linalg.cholesky(gram)
    posterior = jax.scipy.linalg.cho_solve((factor, True), moment)
    resid = jnp.dot(features, posterior, precision=lax.Precision.HIGHEST) - target
    feat_grad = (resid[:, None] * posterior[None, :]).astype(jnp.bfloat16)
    moment_term = contract_rows(hidden.astype(jnp.float32), resid[:, None], lax.Precision.HIGHEST)[
        :, 0
    ]
    row_moment = lax.psum(moment_term, ("grp", "row"))
    num_devices = lax.axis_size("grp") * lax.axis_size("row")
    own_rows = width // num_devices
    linear_index = lax.axis_index("grp") * lax.axis_size("row") + lax.axis_index("row")
    own_moment = lax.dynamic_slice_in_dim(row_moment, linear_index * own_rows, own_rows, 0)
    grad_proj = own_moment[:, None] * posterior[None, :]
    back = lax.dot_general(
        feat_grad, w_proj, (((1,), (1,)), ((), ())), preferred_element_type=jnp.float32
    )
    sigmoid_pre = jax.nn.sigmoid(pre)
    pre_grad = (back * sigmoid_pre * (1.0 + pre * (1.0 - sigmoid_pre))).astype(jnp.bfloat16)
    group_rows = lax.psum_scatter(
        contract_rows(normed, pre_grad), "grp", scatter_dimension=0, tiled=True
    )
    grad_hidden = lax.psum_scatter(group_rows, "row", scatter_dimension=0, tiled=True)
    return (grad_hidden, grad_proj)


def solution(mesh):
    return jax.shard_map(
        body,
        mesh=mesh,
        in_specs=(
            P(("grp", "row"), None),
            P(),
            P(),
            P(),
            P(("grp", "row")),
            P(("grp", "row")),
            P(("grp", "row")),
            P(),
            P(),
        ),
        out_specs=(P(("grp", "row"), None), P(("grp", "row"), None)),
        check_vma=False,
    )
```

profile of v0, /device:TPU:0, one launch (start us, length us, event | category | flops | bytes accessed | tf_op | source)
XLA Modules:
  0.0 453.9 jit_solution(2853332195906063706)
XLA Ops:
  7.2 0.0 copy-start
  7.2 0.0 all-reduce.3.cloned.1.call-start
  7.2 2.2 fusion
  9.4 11.6 %fusion.3 = (bf16[512,2048]{1,0:T(8,128)(2,1)S(1)}, f32[512,2048]{1,0:T(8,128)}) fusion(bf16[512,2048]{1,0:T(8,128)(2,1)} %param.9, bf16[2048,2048]{1,0:T(8,128)(2,1)} %param.11, f32[2048]{0:T(1024)} %param.10, f32[512]{0:T(512)S(1)} %add_rsqrt_fusion), kind=kOutput, calls=%fused_computation.8 | convolution fusion | flops 4306501632 | bytes 16787456 | tf_op jit(solution)/shard_map/dot_general | solution.py:11
  21.0 0.0 copy-start.1
  21.0 0.0 copy-start.6
  21.0 0.0 copy-start.8
  21.0 0.0 copy-start.7
  21.0 0.0 copy-start.3
  21.0 0.0 copy-start.4
  21.0 1.3 copy-done.1
  22.3 0.0 copy-done
  22.3 0.7 fusion.33
  23.0 0.0 copy-start.5
  23.0 1.7 fusion.34
  24.8 0.0 all-reduce.3.cloned.1.call-update
  24.8 0.0 reduce-scatter.3.cloned.1.call-start
  24.8 0.0 copy-done.6
  24.8 0.0 copy-done.8
  24.9 0.6 fusion.10
  25.5 0.0 copy-done.7
  25.5 0.6 fusion.9
  26.1 0.0 copy-done.3
  26.1 0.0 copy-done.4
  26.2 0.3 fusion.35
  26.5 42.2 %psum.22 = f32[256]{0:T(256)S(1)} all-reduce(f32[256]{0:T(256)S(1)} %bitcast.98), channel_id=1, replica_groups=mesh['grp'=4,'row'=8] {'grp','row'}, use_global_device_ids=true, to_apply=%region_6.7 | all-reduce | flops 256 | bytes 2048 | tf_op jit(solution)/shard_map/psum | solution.py:53
  68.7 84.1 %all-reduce.3.cloned.1.call-done = f32[256,256]{0,1:T(8,128)} async-done(((f32[256,256]{0,1:T(8,128)}), f32[256,256]{0,1:T(8,128)}) %all-reduce.3.cloned.1.call-update) | async-done | bytes 262160 | tf_op jit(solution)/shard_map/psum | solution.py:53
  152.8 1.0 convert_add_fusion.1
  153.7 0.1 copy.12
  153.9 1.0 fusion.16
  154.9 11.7 %cholesky.50 = f32[128,128]{1,0:T(8,128)S(1)} custom-call(f32[128,128]{1,0:T(8,128)S(1)} %cholesky.118), custom_call_target="Cholesky" | custom-call | tf_op jit(solution)/shard_map/jit(cholesky)/cholesky | solution.py:55
  166.6 9.8 %custom-call.18 = f32[1,128,128]{1,2,0:T(8,128)S(1)} custom-call(f32[1,128,128]{2,1,0:T(8,128)S(1)} %get-tuple-element.23), custom_call_target="InvertDiagBlocksLowerTriangular" | custom-call | tf_op jit(solution)/shard_map/jit(cholesky)/cholesky | solution.py:55
  176.5 0.2 constant_dynamic-update-slice_fusion.1
  176.7 0.3 convolution_subtract_fusion
  177.0 11.7 %cholesky.105 = f32[128,128]{1,0:T(8,128)S(1)} custom-call(f32[128,128]{1,0:T(8,128)S(1)} %convolution_subtract_fusion), custom_call_target="Cholesky" | custom-call | tf_op jit(solution)/shard_map/jit(cholesky)/cholesky | solution.py:55
  188.7 0.7 compare_reduce_fusion
  190.8 0.1 triangular_solve.73
  190.9 4.1 while.1
  190.9 0.6 fusion.57
  191.5 1.4 bitcast_dynamic-update-slice_fusion.2
  193.0 0.6 fusion.57
  193.5 1.4 bitcast_dynamic-update-slice_fusion.2
  195.0 19.9 %custom-call.19 = f32[2,128,128]{1,2,0:T(8,128)S(1)} custom-call(f32[2,128,128]{2,1,0:T(8,128)S(1)} %get-tuple-element.9), custom_call_target="InvertDiagBlocksLowerTriangular" | custom-call | tf_op jit(solution)/shard_map/jit(_cho_solve)/triangular_solve | solution.py:56
  214.9 0.2 fusion.24
  215.0 0.2 fusion.8
  215.2 0.2 convolution_bitcast_fusion.3
  215.4 0.2 convolution_bitcast_fusion.2
  215.6 0.2 fusion.6
  215.8 0.2 convolution_bitcast_fusion
  216.0 0.6 fusion.31
  216.6 0.0 copy-done.5
  216.7 11.6 %fusion.4 = f32[2048,2048]{1,0:T(8,128)} fusion(f32[512,2048]{1,0:T(8,128)} %get-tuple-element.25, bf16[2048,256]{1,0:T(8,128)(2,1)S(1)} %copy-done, bf16[512,2048]{1,0:T(8,128)(2,1)} %param.9, f32[2048]{0:T(1024)S(1)} %copy-done.5, f32[512]{0:T(512)S(1)} %add_rsqrt_fusion, f32[256]{0:T(256)S(1)} %bitcast.96, f32[512]{0:T(512)S(1)} %sub.14), kind=kOutput, calls=%fused_computation.11 | convolution fusion | flops 4845731840 | bytes 24130560 | tf_op jit(solution)/shard_map/dot_general | solution.py:27
  228.2 0.0 reduce-scatter.3.cloned.1.call-update
  228.3 0.0 copy-start.2
  228.3 0.0 reduce-scatter.5.cloned.1.call-start
  228.3 125.2 %reduce-scatter.3.cloned.1.call-done = f32[512,2048]{1,0:T(8,128)} async-done(((f32[2048,2048]{1,0:T(8,128)}), f32[512,2048]{1,0:T(8,128)}) %reduce-scatter.3.cloned.1.call-update) | async-done | bytes 4194320 | tf_op jit(solution)/shard_map/reduce_scatter | solution.py:73
  353.5 0.0 reduce-scatter.5.cloned.1.call-update
  353.6 0.0 copy-done.2
  353.6 0.9 fusion.36
  354.5 41.8 %psum.23 = f32[2048]{0:T(1024)S(1)} all-reduce(f32[2048]{0:T(1024)S(1)} %bitcast.92), channel_id=1, replica_groups=mesh['grp'=4,'row'=8] {'grp','row'}, use_global_device_ids=true, to_apply=%region_9.10 | all-reduce | flops 2048 | bytes 16384 | tf_op jit(solution)/shard_map/psum | solution.py:62
  396.3 0.1 dynamic_slice.3
  396.4 0.7 broadcast_multiply_fusion
  397.1 50.2 %reduce-scatter.5.cloned.1.call-done = f32[64,2048]{1,0:T(8,128)} async-done(((f32[512,2048]{1,0:T(8,128)}), f32[64,2048]{1,0:T(8,128)}) %reduce-scatter.5.cloned.1.call-update) | async-done | bytes 524304 | tf_op jit(solution)/shard_map/reduce_scatter | solution.py:76
  (13 shorter events, 0.2 us)
Async XLA Ops:
  7.2 15.1 %copy-start = (bf16[2048,256]{1,0:T(8,128)(2,1)S(1)}, bf16[2048,256]{1,0:T(8,128)(2,1)}, u32[]{:S(2)}) copy-start(bf16[2048,256]{1,0:T(8,128)(2,1)} %param.12) | copy-start | bytes 3145732
  7.2 145.6 %all-reduce.3.cloned.1.call-start = ((), (), s32[]{:S(2)}) async-start(), calls=%async_computation.2 | async-start | bytes 524288 | tf_op jit(solution)/shard_map/psum | solution.py:53
  21.0 1.3 copy-start.1
  21.0 3.9 copy-start.6
  21.0 3.9 copy-start.8
  21.0 4.5 copy-start.7
  21.0 5.2 %copy-start.3 = (f32[512]{0:T(512)S(1)}, f32[512]{0:T(512)}, u32[]{:S(2)}) copy-start(f32[512]{0:T(512)} %param.13) | copy-start | bytes 6148
  21.0 5.2 %copy-start.4 = (f32[512]{0:T(512)S(1)}, f32[512]{0:T(512)}, u32[]{:S(2)}) copy-start(f32[512]{0:T(512)} %param.14) | copy-start | bytes 6148
  23.0 193.6 %copy-start.5 = (f32[2048]{0:T(1024)S(1)}, f32[2048]{0:T(1024)}, u32[]{:S(2)}) copy-start(f32[2048]{0:T(1024)} %param.10) | copy-start | bytes 24580
  24.8 328.8 %reduce-scatter.3.cloned.1.call-start = ((), (), s32[]{:S(2)}) async-start(), calls=%async_computation.3 | async-start | bytes 20971520 | tf_op jit(solution)/shard_map/reduce_scatter | solution.py:73
  228.3 125.3 %copy-start.2 = (bf16[512,2048]{1,0:T(8,128)(2,1)S(1)}, bf16[512,2048]{1,0:T(8,128)(2,1)}, u32[]{:S(2)}) copy-start(bf16[512,2048]{1,0:T(8,128)(2,1)} %copy-done.1) | copy-start | bytes 6291460
  228.3 219.1 %reduce-scatter.5.cloned.1.call-start = ((), (), s32[]{:S(2)}) async-start(), calls=%async_computation.4 | async-start | bytes 4718592 | tf_op jit(solution)/shard_map/reduce_scatter | solution.py:76
Sparse Core Ops, SparseCore 0:
  24.9 127.8 all-reduce.2
  228.4 125.1 reduce-scatter.2
  358.2 89.1 reduce-scatter.4
where the time goes:
time: 454 us
  waiting for transfers between devices  260 us (57%)
  blocking collectives  84 us (19%)
  other arithmetic  58.8 us (13%)
  matrix products  30.3 us (7%)
  between operations  15.3 us (3%)
  local copies, waits for them, and re-layouts  5.69 us (1%)
    reduce_scatter x1, waiting for transfers between devices, body(): lax.psum_scatter(contract_rows(normed, pre_grad), 'grp', scatter_dimensio...  125 us
    psum x1, waiting for transfers between devices, body(): gram, moment = lax.psum((gram_part, moment_part), ('grp', 'row'))  84.1 us
    reduce_scatter x1, waiting for transfers between devices, body(): lax.psum_scatter(group_rows, 'row', scatter_dimension=0, tiled=True)  50.2 us
    psum x1, blocking collectives, body(): gram, moment = lax.psum((gram_part, moment_part), ('grp', 'row'))  42.2 us
    psum x1, blocking collectives, body(): row_moment = lax.psum(moment_term, ('grp', 'row'))  41.8 us
    another operation x6, other arithmetic, body(): factor = jnp.linalg.cholesky(gram)  34 us
    another operation x4, other arithmetic, body(): posterior = jax.scipy.linalg.cho_solve((factor, True), moment)  19.9 us
    dot_general x4, matrix products, contract_rows(): lax.dot_general(left, right, (((0,), (0,)), ((), ())), precision=precisio...  14.6 us
  transfers between devices with their start and end apart: 3, of which 3 were waited for; matrix products, arithmetic and copies ran while one was open for 1% of the time, Pallas kernels for 0%

commit v1 on v0

v1 whole, which is shorter than its diff:
```python
import functools

import jax
import jax.numpy as jnp
from jax import lax
from jax.experimental import pallas as pl
from jax.experimental.pallas import tpu as pltpu
from jax.sharding import PartitionSpec as P

HIGH = lax.Precision.HIGHEST
MESH = pl.DeviceIdType.MESH
VMEM = pl.BlockSpec(memory_space=pltpu.VMEM)


def forward(rows_in, norm_gain, w_hidden, w_proj):
    values = rows_in.astype(jnp.float32)
    mean_square = jnp.mean(values * values, axis=1, keepdims=True)
    normed = (values * lax.rsqrt(mean_square + 1e-06) * norm_gain).astype(jnp.bfloat16)
    pre = jnp.dot(normed, w_hidden, preferred_element_type=jnp.float32)
    hidden = (values + jax.nn.silu(pre)).astype(jnp.bfloat16)
    features = jnp.dot(hidden, w_proj, preferred_element_type=jnp.float32)
    return (normed, pre, hidden, features)


def make_target(observed, evolved, station_ids, station_gain, station_offset):
    onehot = (
        station_ids[:, None] == jnp.arange(station_gain.shape[0], dtype=jnp.int32)[None, :]
    ).astype(jnp.float32)
    gain_rows = jnp.dot(onehot, station_gain, precision=HIGH)
    offset_rows = jnp.dot(onehot, station_offset, precision=HIGH)
    return observed - gain_rows * evolved - offset_rows


def contract_rows(left, right, precision=None):
    return lax.dot_general(
        left,
        right,
        (((0,), (0,)), ((), ())),
        precision=precision,
        preferred_element_type=jnp.float32,
    )


def reduce_kernel(groups, rows, part, out, landed, send_a, recv_a, send_b, recv_b):
    count = groups * rows
    me = lax.axis_index("grp") * rows + lax.axis_index("row")

    def peer(step):
        where = lax.rem(me + step, count)
        return where, (where // rows, lax.rem(where, rows))

    barrier = pltpu.get_barrier_semaphore()

    @pl.loop(1, count)
    def _(step):
        pl.semaphore_signal(barrier, inc=1, device_id=peer(step)[1], device_id_type=MESH)

    pl.semaphore_wait(barrier, count - 1)

    def scatter(step):
        where, device = peer(step)
        return pltpu.make_async_remote_copy(
            src_ref=part.at[where],
            dst_ref=landed.at[step],
            send_sem=send_a.at[step],
            recv_sem=recv_a.at[step],
            device_id=device,
            device_id_type=MESH,
        )

    def gather(step):
        return pltpu.make_async_remote_copy(
            src_ref=out.at[me],
            dst_ref=out.at[me],
            send_sem=send_b.at[step],
            recv_sem=recv_b.at[step],
            device_id=peer(step)[1],
            device_id_type=MESH,
        )

    @pl.loop(1, count)
    def _(step):
        scatter(step).start()

    def add(step, total):
        scatter(step).wait_recv()
        return total + landed[step]

    out[me] = lax.fori_loop(1, count, add, part[me])

    @pl.loop(1, count)
    def _(step):
        gather(step).start()

    @pl.loop(1, count)
    def _(step):
        scatter(step).wait_send()
        gather(step).wait()


def reduce_all(part, groups, rows):
    count = groups * rows
    high, wide = part.shape
    blocks = part.reshape(count, high // count, wide)
    out = pl.pallas_call(
        functools.partial(reduce_kernel, groups, rows),
        out_shape=jax.ShapeDtypeStruct(blocks.shape, jnp.float32),
        in_specs=[VMEM],
        out_specs=VMEM,
        scratch_shapes=[pltpu.VMEM(blocks.shape, jnp.float32)]
        + [pltpu.SemaphoreType.DMA((count,))] * 4,
        compiler_params=pltpu.CompilerParams(
            collective_id=0, has_side_effects=True, vmem_limit_bytes=16 * 2**20
        ),
    )(blocks)
    return out.reshape(high, wide)


def solve_kernel(aug, out, work):
    feat, wide = aug.shape
    rows = lax.broadcasted_iota(jnp.int32, (feat, wide), 0)
    columns = lax.broadcasted_iota(jnp.int32, (feat, wide), 1)
    work[...] = aug[...] + jnp.where(rows == columns, 1.0, 0.0)
    tall = 8
    sub = lax.broadcasted_iota(jnp.int32, (tall, 1), 0)
    for k in range(feat // tall):
        low = k * tall
        base = low // 128 * 128
        pivot = work[low : low + tall, base:]
        for i in range(tall):
            lane = low + i - base
            column = pivot[:, lane : lane + 1]
            line = pivot[i : i + 1, :] * (1.0 / column[i : i + 1, :])
            pivot = jnp.where(sub == i, line, pivot - column * line)
        for t in list(range(k + 1, feat // tall)) + list(range(k)):
            here = slice(t * tall, (t + 1) * tall)
            left = work[here, low : low + tall]
            total = work[here, base:]
            for i in range(tall):
                total = total - left[:, i : i + 1] * pivot[i : i + 1, :]
            work[here, base:] = total
        work[low : low + tall, base:] = pivot
    out[...] = work[:, feat:]


def solve(aug):
    feat, wide = aug.shape
    return pl.pallas_call(
        solve_kernel,
        out_shape=jax.ShapeDtypeStruct((feat, wide - feat), jnp.float32),
        in_specs=[VMEM],
        out_specs=VMEM,
        scratch_shapes=[pltpu.VMEM((feat, wide), jnp.float32)],
        compiler_params=pltpu.CompilerParams(vmem_limit_bytes=40 * 2**20),
    )(aug)


def scatter_kernel(side, depth, pieces, left, right, extra, out, extra_out, *scratch):
    main, small, (send_sem, recv_sem) = scratch[:6], scratch[6:12], scratch[12:]
    grp, row = lax.axis_index("grp"), lax.axis_index("row")
    core, x = lax.rem(grp, 2), grp // 2
    z, y = row // side, lax.rem(row, side)
    p = x + core * (y - x)
    q = y + core * (x - y)
    size = out.shape[1] // pieces

    def device(new_p, new_q, new_z, new_core):
        new_x = new_p + core * (new_q - new_p)
        new_y = new_q + core * (new_p - new_q)
        return (new_x * 2 + new_core, new_z * side + new_y)

    hops = [[(0, None, device(p, q, z, 1 - core))], [], [], []]
    for step in range(1, side):
        there = lax.rem(p + step, side)
        hops[1].append((step - 1, there, device(there, q, z, core)))
    for step in range(1, side):
        there = lax.rem(q + step, side)
        hops[2].append((step - 1, there, device(p, there, z, core)))
    for step in range(1, depth):
        there = lax.rem(z + step, depth)
        hops[3].append((step - 1, there, device(p, q, there, core)))

    barrier = pltpu.get_barrier_semaphore()
    for hop in sum(hops, []):
        pl.semaphore_signal(barrier, inc=1, device_id=hop[2], device_id_type=MESH)
    pl.semaphore_wait(barrier, sum(len(stage) for stage in hops))

    def copies(group, piece, stage):
        give, mine, land = group[0], group[1], group[2:]
        sem = pieces if group is small else piece
        number = sum(len(before) for before in hops[:stage])
        result = []
        for slot, there, target in hops[stage]:
            if stage == 0:
                src, dst = give.at[piece], land[0].at[piece]
            elif stage == 1:
                src, dst = mine.at[piece, there], land[1].at[piece, slot]
            elif stage == 2:
                src, dst = mine.at[piece, p, there], land[2].at[piece, slot]
            else:
                src, dst = mine.at[piece, p, q, there], land[3].at[piece, slot]
            result.append(
                pltpu.make_async_remote_copy(
                    src_ref=src,
                    dst_ref=dst,
                    send_sem=send_sem.at[sem, number + slot],
                    recv_sem=recv_sem.at[sem, number + slot],
                    device_id=target,
                    device_id_type=MESH,
                )
            )
        return result

    def begin(group, piece, stage):
        for copy in copies(group, piece, stage):
            copy.start()

    def finish(group, piece, stage):
        mine, land = group[1], group[2:]
        for copy in copies(group, piece, stage):
            copy.wait_recv()
        if stage == 0:
            mine[piece] = mine[piece] + land[0][piece]
        elif stage == 1:
            for slot in range(side - 1):
                mine[piece, p] = mine[piece, p] + land[1][piece, slot]
        elif stage == 2:
            for slot in range(side - 1):
                mine[piece, p, q] = mine[piece, p, q] + land[2][piece, slot]
        else:
            total = mine[piece, p, q, z]
            for slot in range(depth - 1):
                total = total + land[3][piece, slot]
            if group is small:
                extra_out[...] = total
            else:
                out[:, pl.ds(pl.multiple_of(piece * size, size), size)] = total
        if stage < 3:
            begin(group, piece, stage + 1)

    def product(half, piece, into):
        columns = pl.ds(pl.multiple_of(piece * size, size), size)
        into[piece] = jnp.dot(
            left[half], right[:, columns], preferred_element_type=jnp.float32
        ).reshape(into.shape[1:])

    small[0][0] = extra[1 - core]
    small[1][0] = extra[core]
    begin(small, 0, 0)

    @pl.loop(0, pieces)
    def _(piece):
        product(1 - core, piece, main[0])
        begin(main, piece, 0)
        product(core, piece, main[1])

        @pl.when(piece > 0)
        def _():
            finish(main, piece - 1, 0)

    finish(main, pieces - 1, 0)
    finish(small, 0, 0)
    finish(small, 0, 1)

    @pl.loop(0, pieces)
    def _(piece):
        finish(main, piece, 1)

        @pl.when(piece > 0)
        def _():
            finish(main, piece - 1, 2)

    finish(main, pieces - 1, 2)
    finish(small, 0, 2)
    finish(small, 0, 3)

    @pl.loop(0, pieces)
    def _(piece):
        finish(main, piece, 3)

    for stage in range(4):
        for copy in copies(small, 0, stage):
            copy.wait_send()

    @pl.loop(0, pieces)
    def _(piece):
        for stage in range(4):
            for copy in copies(main, piece, stage):
                copy.wait_send()


def order_rows(array, side, depth):
    tail = array.shape[1:]
    split = array.reshape((side, 2, depth, side, -1) + tail)
    rest = tuple(range(3, split.ndim - 1))
    first = jnp.transpose(split[:, 0], (0, 2, 1) + rest)
    second = jnp.transpose(split[:, 1], (2, 0, 1) + rest)
    return jnp.stack([first, second])


def scatter_sum(normed, pre_grad, moment_term, groups, rows):
    side = groups // 2
    depth = rows // side
    own = normed.shape[1] // (groups * rows)
    width = pre_grad.shape[1]
    pieces = width // 256
    left = order_rows(normed.T, side, depth).reshape(2, -1, normed.shape[0])
    extra = order_rows(moment_term, side, depth)[..., None, :]
    extra = jnp.pad(extra, [(0, 0)] * 4 + [(0, 7), (0, 128 - own)])

    def stage_buffers(count, high, wide):
        full = (count, side, side, depth, high, wide)
        shapes = [full] * 3 + [
            (count, side - 1, side, depth, high, wide),
            (count, side - 1, depth, high, wide),
            (count, depth - 1, high, wide),
        ]
        return [pltpu.VMEM(shape, jnp.float32) for shape in shapes]

    number = 1 + 2 * (side - 1) + depth - 1
    return pl.pallas_call(
        functools.partial(scatter_kernel, side, depth, pieces),
        out_shape=(
            jax.ShapeDtypeStruct((own, width), jnp.float32),
            jax.ShapeDtypeStruct((8, 128), jnp.float32),
        ),
        in_specs=[VMEM] * 3,
        out_specs=(VMEM, VMEM),
        scratch_shapes=stage_buffers(pieces, own, width // pieces)
        + stage_buffers(1, 8, 128)
        + [pltpu.SemaphoreType.DMA((pieces + 1, number))] * 2,
        compiler_params=pltpu.CompilerParams(
            collective_id=1, has_side_effects=True, vmem_limit_bytes=56 * 2**20
        ),
    )(left, pre_grad, extra)


def body(
    inputs,
    norm_gain,
    w_hidden,
    w_proj,
    observed,
    evolved,
    station_ids,
    station_gain,
    station_offset,
):
    groups, rows = lax.axis_size("grp"), lax.axis_size("row")
    feat_width = w_proj.shape[1]
    normed, pre, hidden, features = forward(inputs, norm_gain, w_hidden, w_proj)
    target = make_target(observed, evolved, station_ids, station_gain, station_offset)
    wide = jnp.concatenate(
        [features, jnp.broadcast_to(target[:, None], (target.shape[0], 128))], axis=1
    )
    aug = reduce_all(contract_rows(features, wide, HIGH), groups, rows)
    posterior = solve(aug)[:, 0]
    resid = jnp.dot(features, posterior, precision=HIGH) - target
    direction = jnp.dot(w_proj.astype(jnp.float32), posterior, precision=HIGH)
    moment_term = contract_rows(hidden.astype(jnp.float32), resid[:, None], HIGH)[:, 0]
    sigmoid_pre = jax.nn.sigmoid(pre)
    slope = sigmoid_pre * (1.0 + pre * (1.0 - sigmoid_pre))
    pre_grad = (resid[:, None] * direction[None, :] * slope).astype(jnp.bfloat16)
    grad_hidden, moment = scatter_sum(normed, pre_grad, moment_term, groups, rows)
    own_moment = moment[0, : grad_hidden.shape[0]]
    grad_proj = own_moment[:, None] * posterior[None, :]
    return (grad_hidden, grad_proj)


def solution(mesh):
    return jax.shard_map(
        body,
        mesh=mesh,
        in_specs=(
            P(("grp", "row"), None),
            P(),
            P(),
            P(),
            P(("grp", "row")),
            P(("grp", "row")),
            P(("grp", "row")),
            P(),
            P(),
        ),
        out_specs=(P(("grp", "row"), None), P(("grp", "row"), None)),
        check_vma=False,
    )
```

time: 454 us -> 205 us (0.45)
  waiting for transfers between devices: 260 us -> 0 us
  Pallas kernels: 0 us -> 164 us
  blocking collectives: 84 us -> 0 us
  other arithmetic: 58.8 us -> 10.8 us
  between operations: 15.3 us -> 0.88 us
  matrix products: 30.3 us -> 17 us
  local copies, waits for them, and re-layouts: 5.69 us -> 11.9 us
    reduce_scatter x2 -> x0, waiting for transfers between devices: 175 us -> none  [the longest x1 125 us: body(): lax.psum_scatter(contract_rows(normed, pre_grad), 'grp', scatter_dimensio...]
    pallas_call x0 -> x3, Pallas kernels: none -> 164 us  [the longest x1 108 us: scatter_sum(): pl.pallas_call(functools.partial(scatter_kernel, side, depth, pieces), ou...]
    psum x1 -> x0, waiting for transfers between devices: 84.1 us -> none  [body(): gram, moment = lax.psum((gram_part, moment_part), ('grp', 'row'))]
    psum x2 -> x0, blocking collectives: 84 us -> none  [the longest x1 42.2 us: body(): gram, moment = lax.psum((gram_part, moment_part), ('grp', 'row'))]
    another operation x10 -> x2, other arithmetic: 54 us -> 1.54 us  [order_rows(): return jnp.stack([first, second])]
    dot_general x4 -> x2, matrix products: 14.6 us -> 5.13 us  [contract_rows(): lax.dot_general(left, right, (((0,), (0,)), ((), ())), precision=precisio...]
    convert_element_type x0 -> x2, other arithmetic: none -> 6.37 us  [the longest x1 4.39 us: body(): (resid[:, None] * direction[None, :] * slope).astype(jnp.bfloat16)]
  transfers between devices with their start and end apart: 3 -> 0, of which waited for: 3 -> 0; matrix products, arithmetic and copies ran while one was open for 1% -> 0% of each run, Pallas kernels for 0% -> 0%
where the time goes in v1:
time: 205 us
  Pallas kernels  164 us (80%)
  matrix products  17 us (8%)
  local copies, waits for them, and re-layouts  11.9 us (6%)
  other arithmetic  10.8 us (5%)
    pallas_call x1, Pallas kernels, scatter_sum(): pl.pallas_call(functools.partial(scatter_kernel, side, depth, pieces), ou...  108 us
    pallas_call x1, Pallas kernels, reduce_all(): pl.pallas_call(functools.partial(reduce_kernel, groups, rows), out_shape=...  29.5 us
    pallas_call x1, Pallas kernels, solve(): pl.pallas_call(solve_kernel, out_shape=jax.ShapeDtypeStruct((feat, wide -...  26.2 us
    dot_general x1, matrix products, forward(): pre = jnp.dot(normed, w_hidden, preferred_element_type=jnp.float32)  8.57 us
    dot_general x2, matrix products, contract_rows(): lax.dot_general(left, right, (((0,), (0,)), ((), ())), precision=precisio...  5.13 us
    convert_element_type x1, other arithmetic, body(): (resid[:, None] * direction[None, :] * slope).astype(jnp.bfloat16)  4.39 us

profile of v1, /device:TPU:0, one launch (start us, length us, event | category | flops | bytes accessed | tf_op | source)
XLA Modules:
  0.0 204.5 jit_solution(8983506698996908595)
XLA Ops:
  0.6 0.0 copy-start
  0.6 2.2 %fusion = f32[512]{0:T(512)S(1)} fusion(bf16[512,2048]{1,0:T(8,128)(2,1)} %param.9), kind=kLoop, calls=%fused_computation.3 | loop fusion | flops 3145216 | bytes 2099200 | tf_op jit(solution)/shard_map/reduce_sum | solution.py:17
  2.8 0.0 copy-start.2
  2.8 0.0 copy-start.4
  2.8 8.6 %fusion.9 = f32[512,2048]{1,0:T(8,128)S(1)} fusion(bf16[2048,2048]{1,0:T(8,128)(2,1)} %param.11, bf16[512,2048]{1,0:T(8,128)(2,1)} %param.9, f32[2048]{0:T(1024)} %param.10, f32[512]{0:T(512)S(1)} %add_rsqrt_fusion), kind=kOutput, calls=%fused_computation.19 | convolution fusion | flops 4299161600 | bytes 14690304 | tf_op jit(solution)/shard_map/dot_general | solution.py:19
  11.4 0.0 copy-done.2
  11.4 0.0 copy-done.4
  11.4 0.0 copy-start.1
  11.5 0.0 copy-start.7
  11.5 0.0 copy-start.8
  11.5 0.0 copy-start.9
  11.5 2.0 fusion.3
  13.5 0.0 copy-done.1
  13.5 0.0 copy-start.3
  13.5 0.0 copy-start.5
  13.5 0.0 copy-start.6
  13.5 0.0 copy-done
  13.5 0.8 fusion.15
  14.3 0.0 copy-done.7
  14.3 0.0 copy-done.8
  14.3 0.6 fusion.4
  14.9 0.0 copy-done.9
  14.9 0.6 fusion.5
  15.6 0.0 copy-done.5
  15.6 0.0 copy-done.6
  15.7 1.0 convolution_bitcast_fusion.part
  16.7 29.5 %shard_map.104 = f32[32,8,384]{2,1,0:T(8,128)S(1)} custom-call(f32[32,8,384]{2,1,0:T(8,128)S(1)} %convolution_bitcast_fusion.part), custom_call_target="tpu_custom_call" | custom-call | tf_op jit(solution)/shard_map/pallas_call | solution.py:105
  46.1 26.2 %shard_map.105 = f32[256,128]{1,0:T(8,128)S(1)} custom-call(f32[256,384]{1,0:T(8,128)S(1)} %bitcast.58), custom_call_target="tpu_custom_call" | custom-call | tf_op jit(solution)/shard_map/pallas_call | solution.py:148
  72.4 0.1 slice_reduce_fusion
  72.5 0.0 copy-done.3
  72.5 0.4 fusion.16
  72.9 4.0 %copy.17 = bf16[2048,512]{1,0:T(8,128)(2,1)} copy(bf16[2048,512]{0,1:T(8,128)(2,1)} %bitcast.59) | data formatting | bytes 4194304 | tf_op jit(solution)/shard_map/dot_general | solution.py:35
  76.9 4.1 %fusion.18 = f32[1,2,2,4,2,64]{5,0,4,3,2,1:T(1,128)S(1)} fusion(bf16[2,2,4,2,64,512]{5,4,3,2,1,0:T(8,128)(2,1)} %bitcast.61, f32[512,1,1,1,1,1]{0,1,5,4,3,2:T(1,128)S(1)} %bitcast.67), kind=kOutput, calls=%fused_computation.36 | convolution fusion | flops 12582912 | bytes 2107392 | tf_op jit(solution)/shard_map/dot_general | solution.py:35
  81.0 0.7 pad.4.extra
  81.7 0.9 fusion.17
  82.6 4.4 %multiply_convert_fusion.right = bf16[512,2048]{1,0:T(8,128)(2,1)} fusion(f32[512,2048]{1,0:T(8,128)} %copy-done.1, f32[2048]{0:T(1024)S(1)} %bitcast.66, f32[512]{0:T(512)S(1)} %sub.14), kind=kLoop, calls=%fused_computation.7 | loop fusion | flops 10485760 | bytes 6301696 | tf_op jit(solution)/shard_map/convert_element_type | solution.py:363
  87.0 2.5 %copy.14 = bf16[2048,512]{1,0:T(8,128)(2,1)} copy(bf16[2048,512]{0,1:T(8,128)(2,1)S(1)} %get-tuple-element.7) | data formatting | bytes 4194304 | tf_op jit(solution)/shard_map/transpose | solution.py:307
  89.5 1.8 slice_bitcast_fusion.1
  91.3 0.1 copy.15
  91.4 0.1 copy.16
  91.5 1.5 pad_maximum_fusion.left
  93.0 108.3 %shard_map.106 = (f32[64,2048]{1,0:T(8,128)}, f32[8,128]{1,0:T(8,128)}) custom-call(bf16[2,1024,512]{2,1,0:T(8,128)(2,1)} %pad_maximum_fusion.left, bf16[512,2048]{1,0:T(8,128)(2,1)} %multiply_convert_fusion.right, f32[2,2,2,4,8,128]{5,4,3,2,1,0:T(8,128)} %pad.4.extra), custom_call_target="tpu_custom_call" | custom-call | tf_op jit(solution)/shard_map/pallas_call | solution.py:321
  201.3 0.7 slice_bitcast_fusion.4
  202.0 0.7 broadcast_multiply_fusion
  202.7 1.9 copy.26
  (7 shorter events, 0.1 us)
Async XLA Ops:
  0.6 12.9 %copy-start = (bf16[2048,256]{1,0:T(8,128)(2,1)S(1)}, bf16[2048,256]{1,0:T(8,128)(2,1)}, u32[]{:S(2)}) copy-start(bf16[2048,256]{1,0:T(8,128)(2,1)} %param.12) | copy-start | bytes 3145732
  2.8 8.6 %copy-start.2 = (bf16[512,2048]{1,0:T(8,128)(2,1)S(1)}, bf16[512,2048]{1,0:T(8,128)(2,1)}, u32[]{:S(2)}) copy-start(bf16[512,2048]{1,0:T(8,128)(2,1)} %param.9) | copy-start | bytes 6291460
  2.8 8.6 %copy-start.4 = (f32[2048]{0:T(1024)S(1)}, f32[2048]{0:T(1024)}, u32[]{:S(2)}) copy-start(f32[2048]{0:T(1024)} %param.10) | copy-start | bytes 24580
  11.4 2.0 copy-start.1
  11.5 2.8 %copy-start.7 = (f32[512]{0:T(512)S(1)}, f32[512]{0:T(512)}, u32[]{:S(2)}) copy-start(f32[512]{0:T(512)} %param.17) | copy-start | bytes 6148
  11.5 2.8 %copy-start.8 = (s32[512]{0:T(512)S(1)}, s32[512]{0:T(512)}, u32[]{:S(2)}) copy-start(s32[512]{0:T(512)} %param.15) | copy-start | bytes 6148
  11.5 3.5 %copy-start.9 = (f32[512]{0:T(512)S(1)}, f32[512]{0:T(512)}, u32[]{:S(2)}) copy-start(f32[512]{0:T(512)} %param.16) | copy-start | bytes 6148
  13.5 59.0 %copy-start.3 = (bf16[512,2048]{1,0:T(8,128)(2,1)}, bf16[512,2048]{1,0:T(8,128)(2,1)S(1)}, u32[]{:S(2)}) copy-start(bf16[512,2048]{1,0:T(8,128)(2,1)S(1)} %get-tuple-element.6) | copy-start | bytes 6291460
  13.5 2.1 %copy-start.5 = (f32[512]{0:T(512)S(1)}, f32[512]{0:T(512)}, u32[]{:S(2)}) copy-start(f32[512]{0:T(512)} %param.13) | copy-start | bytes 6148
  13.5 2.1 %copy-start.6 = (f32[512]{0:T(512)S(1)}, f32[512]{0:T(512)}, u32[]{:S(2)}) copy-start(f32[512]{0:T(512)} %param.14) | copy-start | bytes 6148

commit v2 on v1

--- a/solution.py
+++ b/solution.py
@@ -31,6 +31,15 @@
     return observed - gain_rows * evolved - offset_rows
 
 
+def parts_of(vector):
+    parts = []
+    for _ in range(3):
+        parts.append(lax.reduce_precision(vector, 8, 7))
+        vector = vector - parts[-1]
+    parts += [jnp.zeros_like(vector)] * 5
+    return jnp.stack(parts).astype(jnp.bfloat16)
+
+
 def contract_rows(left, right, precision=None):
     return lax.dot_general(
         left,
@@ -41,44 +50,50 @@
     )
 
 
-def reduce_kernel(groups, rows, part, out, landed, send_a, recv_a, send_b, recv_b):
-    count = groups * rows
-    me = lax.axis_index("grp") * rows + lax.axis_index("row")
+def reduce_kernel(groups, rows, part, out, half, landed, pair_sem, sems):
+    chips = groups // 2 * rows
+    grp, row = lax.axis_index("grp"), lax.axis_index("row")
+    core = lax.rem(grp, 2)
+    chip = grp // 2 * rows + row
+    sibling = (grp + 1 - 2 * core, row)
 
     def peer(step):
-        where = lax.rem(me + step, count)
-        return where, (where // rows, lax.rem(where, rows))
+        where = lax.rem(chip + step, chips)
+        return where, (where // rows * 2 + core, lax.rem(where, rows))
 
     barrier = pltpu.get_barrier_semaphore()
-
-    @pl.loop(1, count)
+    pl.semaphore_signal(barrier, inc=1, device_id=sibling, device_id_type=MESH)
+
+    @pl.loop(1, chips)
     def _(step):
         pl.semaphore_signal(barrier, inc=1, device_id=peer(step)[1], device_id_type=MESH)
 
-    pl.semaphore_wait(barrier, count - 1)
-
-    def scatter(step):
-        where, device = peer(step)
+    pl.semaphore_wait(barrier, chips)
+
+    def copy(src, dst, send_sem, recv_sem, device):
         return pltpu.make_async_remote_copy(
-            src_ref=part.at[where],
-            dst_ref=landed.at[step],
-            send_sem=send_a.at[step],
-            recv_sem=recv_a.at[step],
+            src_ref=src,
+            dst_ref=dst,
+            send_sem=send_sem,
+            recv_sem=recv_sem,
             device_id=device,
             device_id_type=MESH,
         )
 
+    def scatter(step):
+        where, device = peer(step)
+        return copy(half.at[where], landed.at[step], sems.at[0, step], sems.at[1, step], device)
+
     def gather(step):
-        return pltpu.make_async_remote_copy(
-            src_ref=out.at[me],
-            dst_ref=out.at[me],
-            send_sem=send_b.at[step],
-            recv_sem=recv_b.at[step],
-            device_id=peer(step)[1],
-            device_id_type=MESH,
-        )
-
-    @pl.loop(1, count)
+        own = out.at[core, chip]
+        return copy(own, own, sems.at[2, step], sems.at[3, step], peer(step)[1])
+
+    first = copy(part.at[1 - core], half, pair_sem.at[0], pair_sem.at[1], sibling)
+    first.start()
+    first.wait_recv()
+    half[...] = half[...] + part[core]
+
+    @pl.loop(1, chips)
     def _(step):
         scatter(step).start()
 
@@ -86,29 +101,39 @@
         scatter(step).wait_recv()
         return total + landed[step]
 
-    out[me] = lax.fori_loop(1, count, add, part[me])
-
-    @pl.loop(1, count)
+    out[core, chip] = lax.fori_loop(1, chips, add, half[chip])
+
+    @pl.loop(1, chips)
     def _(step):
         gather(step).start()
 
-    @pl.loop(1, count)
+    @pl.loop(1, chips)
+    def _(step):
+        gather(step).wait_recv()
+
+    last = copy(out.at[core], out.at[core], pair_sem.at[2], pair_sem.at[3], sibling)
+    last.start()
+
+    @pl.loop(1, chips)
     def _(step):
         scatter(step).wait_send()
-        gather(step).wait()
+        gather(step).wait_send()
+
+    first.wait_send()
+    last.wait()
 
 
 def reduce_all(part, groups, rows):
-    count = groups * rows
+    chips = groups // 2 * rows
     high, wide = part.shape
-    blocks = part.reshape(count, high // count, wide)
+    blocks = part.reshape(2, chips, high // (2 * chips), wide)
     out = pl.pallas_call(
         functools.partial(reduce_kernel, groups, rows),
         out_shape=jax.ShapeDtypeStruct(blocks.shape, jnp.float32),
         in_specs=[VMEM],
         out_specs=VMEM,
-        scratch_shapes=[pltpu.VMEM(blocks.shape, jnp.float32)]
-        + [pltpu.SemaphoreType.DMA((count,))] * 4,
+        scratch_shapes=[pltpu.VMEM(blocks.shape[1:], jnp.float32)] * 2
+        + [pltpu.SemaphoreType.DMA((4,)), pltpu.SemaphoreType.DMA((4, chips))],
         compiler_params=pltpu.CompilerParams(
             collective_id=0, has_side_effects=True, vmem_limit_bytes=16 * 2**20
         ),
@@ -155,7 +180,9 @@
     )(aug)
 
 
-def scatter_kernel(side, depth, pieces, left, right, extra, out, extra_out, *scratch):
+def scatter_kernel(
+    side, depth, pieces, left, pre, resid, direction, extra, out, extra_out, right, *scratch
+):
     main, small, (send_sem, recv_sem) = scratch[:6], scratch[6:12], scratch[12:]
     grp, row = lax.axis_index("grp"), lax.axis_index("row")
     core, x = lax.rem(grp, 2), grp // 2
@@ -239,9 +266,8 @@
             begin(group, piece, stage + 1)
 
     def product(half, piece, into):
-        columns = pl.ds(pl.multiple_of(piece * size, size), size)
         into[piece] = jnp.dot(
-            left[half], right[:, columns], preferred_element_type=jnp.float32
+            left[half], right[...], preferred_element_type=jnp.float32
         ).reshape(into.shape[1:])
 
     small[0][0] = extra[1 - core]
@@ -250,6 +276,11 @@
 
     @pl.loop(0, pieces)
     def _(piece):
+        columns = pl.ds(pl.multiple_of(piece * size, size), size)
+        value = pre[:, columns]
+        sigmoid = 1.0 / (1.0 + jnp.exp(-value))
+        slope = sigmoid * (1.0 + value * (1.0 - sigmoid))
+        right[...] = (resid[...] * direction[:, columns] * slope).astype(jnp.bfloat16)
         product(1 - core, piece, main[0])
         begin(main, piece, 0)
         product(core, piece, main[1])
@@ -298,12 +329,12 @@
     return jnp.stack([first, second])
 
 
-def scatter_sum(normed, pre_grad, moment_term, groups, rows):
+def scatter_sum(normed, pre, resid, direction, moment_term, groups, rows):
     side = groups // 2
     depth = rows // side
     own = normed.shape[1] // (groups * rows)
-    width = pre_grad.shape[1]
-    pieces = width // 256
+    width = pre.shape[1]
+    pieces = width // 128
     left = order_rows(normed.T, side, depth).reshape(2, -1, normed.shape[0])
     extra = order_rows(moment_term, side, depth)[..., None, :]
     extra = jnp.pad(extra, [(0, 0)] * 4 + [(0, 7), (0, 128 - own)])
@@ -324,15 +355,16 @@
             jax.ShapeDtypeStruct((own, width), jnp.float32),
             jax.ShapeDtypeStruct((8, 128), jnp.float32),
         ),
-        in_specs=[VMEM] * 3,
+        in_specs=[VMEM] * 5,
         out_specs=(VMEM, VMEM),
-        scratch_shapes=stage_buffers(pieces, own, width // pieces)
+        scratch_shapes=[pltpu.VMEM((pre.shape[0], width // pieces), jnp.bfloat16)]
+        + stage_buffers(pieces, own, width // pieces)
         + stage_buffers(1, 8, 128)
         + [pltpu.SemaphoreType.DMA((pieces + 1, number))] * 2,
         compiler_params=pltpu.CompilerParams(
             collective_id=1, has_side_effects=True, vmem_limit_bytes=56 * 2**20
         ),
-    )(left, pre_grad, extra)
+    )(left, pre, resid[:, None], direction[None, :], extra)
 
 
 def body(
@@ -356,12 +388,18 @@
     aug = reduce_all(contract_rows(features, wide, HIGH), groups, rows)
     posterior = solve(aug)[:, 0]
     resid = jnp.dot(features, posterior, precision=HIGH) - target
-    direction = jnp.dot(w_proj.astype(jnp.float32), posterior, precision=HIGH)
-    moment_term = contract_rows(hidden.astype(jnp.float32), resid[:, None], HIGH)[:, 0]
-    sigmoid_pre = jax.nn.sigmoid(pre)
-    slope = sigmoid_pre * (1.0 + pre * (1.0 - sigmoid_pre))
-    pre_grad = (resid[:, None] * direction[None, :] * slope).astype(jnp.bfloat16)
-    grad_hidden, moment = scatter_sum(normed, pre_grad, moment_term, groups, rows)
+    direction = jnp.sum(
+        lax.dot_general(
+            parts_of(posterior), w_proj, (((1,), (1,)), ((), ())), preferred_element_type=jnp.float32
+        ),
+        axis=0,
+    )
+    moment_term = jnp.sum(
+        jnp.dot(parts_of(resid), hidden, preferred_element_type=jnp.float32), axis=0
+    )
+    grad_hidden, moment = scatter_sum(
+        normed, pre, resid, direction, moment_term, groups, rows
+    )
     own_moment = moment[0, : grad_hidden.shape[0]]
     grad_proj = own_moment[:, None] * posterior[None, :]
     return (grad_hidden, grad_proj)

time: 205 us -> 189 us (0.922)
  Pallas kernels: 164 us -> 157 us
  other arithmetic: 10.8 us -> 6.41 us
  local copies, waits for them, and re-layouts: 11.9 us -> 8.89 us
    pallas_call x1, Pallas kernels: 29.5 us -> 21.9 us  [reduce_all(): pl.pallas_call(functools.partial(reduce_kernel, groups, rows), out_shape=...]
    convert_element_type x1 -> x0, other arithmetic: 4.39 us -> none  [body(): (resid[:, None] * direction[None, :] * slope).astype(jnp.bfloat16)]
    dot_general x2 -> x1, matrix products: 5.13 us -> 1.02 us  [contract_rows(): lax.dot_general(left, right, (((0,), (0,)), ((), ())), precision=precisio...]
    dot_general x2 -> x0, local copies, waits for them, and re-layouts: 3.99 us -> none  [contract_rows(): lax.dot_general(left, right, (((0,), (0,)), ((), ())), precision=precisio...]
    dot_general x1 -> x2, matrix products: 0.91 us -> 2.97 us  [the longest x1 1.98 us: body(): jnp.dot(parts_of(resid), hidden, preferred_element_type=jnp.float32)]
where the time goes in v2:
time: 189 us
  Pallas kernels  157 us (83%)
  matrix products  15 us (8%)
  local copies, waits for them, and re-layouts  8.89 us (5%)
  other arithmetic  6.41 us (3%)
    pallas_call x1, Pallas kernels, scatter_sum(): pl.pallas_call(functools.partial(scatter_kernel, side, depth, pieces), ou...  109 us
    pallas_call x1, Pallas kernels, solve(): pl.pallas_call(solve_kernel, out_shape=jax.ShapeDtypeStruct((feat, wide -...  26.2 us
    pallas_call x1, Pallas kernels, reduce_all(): pl.pallas_call(functools.partial(reduce_kernel, groups, rows), out_shape=...  21.9 us
    dot_general x1, matrix products, forward(): pre = jnp.dot(normed, w_hidden, preferred_element_type=jnp.float32)  8.57 us

profile of v2, /device:TPU:0, one launch (start us, length us, event | category | flops | bytes accessed | tf_op | source)
XLA Modules:
  0.0 188.7 jit_solution(1311279711257267396)
XLA Ops:
  0.6 0.0 copy-start
  0.6 2.2 %fusion = f32[512]{0:T(512)S(1)} fusion(bf16[512,2048]{1,0:T(8,128)(2,1)} %param.9), kind=kLoop, calls=%fused_computation.3 | loop fusion | flops 3145216 | bytes 2099200 | tf_op jit(solution)/shard_map/reduce_sum | solution.py:17
  2.8 0.0 copy-start.2
  2.8 0.0 copy-start.4
  2.8 8.6 %fusion.10.pre = f32[512,2048]{1,0:T(8,128)S(1)} fusion(bf16[2048,2048]{1,0:T(8,128)(2,1)} %param.11, bf16[512,2048]{1,0:T(8,128)(2,1)} %param.9, f32[2048]{0:T(1024)} %param.10, f32[512]{0:T(512)S(1)} %add_rsqrt_fusion), kind=kOutput, calls=%fused_computation.19 | convolution fusion | flops 4299161600 | bytes 14690304 | tf_op jit(solution)/shard_map/dot_general | solution.py:19
  11.4 0.0 copy-done.2
  11.4 0.0 copy-done.4
  11.4 0.0 copy-start.1
  11.5 0.0 copy-start.7
  11.5 0.0 copy-start.8
  11.5 0.0 copy-start.9
  11.5 2.0 %fusion.3 = (bf16[512,2048]{1,0:T(8,128)(2,1)S(1)}, bf16[2048,512]{0,1:T(8,128)(2,1)S(1)}) fusion(bf16[512,2048]{1,0:T(8,128)(2,1)S(1)} %copy-done.2, f32[512,2048]{1,0:T(8,128)S(1)} %fusion.10.pre, f32[2048]{0:T(1024)S(1)} %copy-done.4, f32[512]{0:T(512)S(1)} %add_rsqrt_fusion), kind=kLoop, calls=%fused_computation.6 | loop fusion | flops 10485760 | bytes 10496000 | tf_op jit(solution)/shard_map/convert_element_type | solution.py:20
  13.5 0.0 copy-done.1
  13.5 0.0 copy-start.3
  13.5 0.0 copy-start.5
  13.5 0.0 copy-start.6
  13.5 0.0 copy-done
  13.5 0.8 fusion.21
  14.3 0.0 copy-done.7
  14.3 0.0 copy-done.8
  14.3 0.6 fusion.4
  15.0 0.0 copy-done.9
  15.0 0.6 fusion.5
  15.6 0.0 copy-done.5
  15.6 0.0 copy-done.6
  15.7 1.0 fusion.6
  16.7 21.9 %shard_map.104 = f32[2,16,8,384]{3,2,1,0:T(8,128)S(1)} custom-call(f32[2,16,8,384]{3,2,1,0:T(8,128)S(1)} %bitcast.54), custom_call_target="tpu_custom_call" | custom-call | tf_op jit(solution)/shard_map/pallas_call | solution.py:130
  38.5 0.0 copy-done.3
  38.6 26.2 %shard_map.105 = f32[256,128]{1,0:T(8,128)S(1)} custom-call(f32[256,384]{1,0:T(8,128)S(1)} %bitcast.53), custom_call_target="tpu_custom_call" | custom-call | tf_op jit(solution)/shard_map/pallas_call | solution.py:173
  64.8 0.1 slice_reduce_fusion
  64.9 0.4 fusion.22
  65.4 2.0 %convolution_reduce_fusion = f32[2048]{0:T(1024)S(1)} fusion(bf16[8,512]{1,0:T(8,128)(2,1)S(1)} %stack.56, bf16[512,2048]{1,0:T(8,128)(2,1)} %copy-done.3), kind=kOutput, calls=%fused_computation.8 | convolution fusion | flops 16791552 | bytes 2113536 | tf_op jit(solution)/shard_map/dot_general | solution.py:398
  67.4 0.1 reshape.76
  67.5 0.7 pad.4.extra
  68.2 1.0 convolution_reduce_fusion.1
  69.2 0.9 copy.19.resid
  70.1 2.5 %copy.14 = bf16[2048,512]{1,0:T(8,128)(2,1)} copy(bf16[2048,512]{0,1:T(8,128)(2,1)S(1)} %get-tuple-element.9) | data formatting | bytes 4194304 | tf_op jit(solution)/shard_map/transpose | solution.py:338
  72.6 1.8 slice_bitcast_fusion.1
  74.4 0.1 copy.15
  74.5 0.1 copy.16
  74.6 1.5 pad_maximum_fusion.left
  76.1 109.4 %shard_map.106 = (f32[64,2048]{1,0:T(8,128)}, f32[8,128]{1,0:T(8,128)}) custom-call(bf16[2,1024,512]{2,1,0:T(8,128)(2,1)} %pad_maximum_fusion.left, f32[512,2048]{1,0:T(8,128)} %copy-done.1, f32[512,1]{1,0:T(8,128)} %copy.19.resid, f32[1,2048]{1,0:T(1,128)} %bitcast.59, f32[2,2,2,4,8,128]{5,4,3,2,1,0:T(8,128)} %pad.4.extra), custom_call_target="tpu_custom_call" | custom-call | tf_op jit(solution)/shard_map/pallas_call | solution.py:352
  185.5 0.7 slice_bitcast_fusion.2
  186.1 0.7 broadcast_multiply_fusion
  186.9 1.9 copy.27
  (19 shorter events, 0.2 us)
Async XLA Ops:
  0.6 12.9 %copy-start = (bf16[2048,256]{1,0:T(8,128)(2,1)S(1)}, bf16[2048,256]{1,0:T(8,128)(2,1)}, u32[]{:S(2)}) copy-start(bf16[2048,256]{1,0:T(8,128)(2,1)} %param.12) | copy-start | bytes 3145732
  2.8 8.6 %copy-start.2 = (bf16[512,2048]{1,0:T(8,128)(2,1)S(1)}, bf16[512,2048]{1,0:T(8,128)(2,1)}, u32[]{:S(2)}) copy-start(bf16[512,2048]{1,0:T(8,128)(2,1)} %param.9) | copy-start | bytes 6291460
  2.8 8.6 %copy-start.4 = (f32[2048]{0:T(1024)S(1)}, f32[2048]{0:T(1024)}, u32[]{:S(2)}) copy-start(f32[2048]{0:T(1024)} %param.10) | copy-start | bytes 24580
  11.4 2.0 %copy-start.1 = (f32[512,2048]{1,0:T(8,128)}, f32[512,2048]{1,0:T(8,128)S(1)}, u32[]{:S(2)}) copy-start(f32[512,2048]{1,0:T(8,128)S(1)} %fusion.10.pre) | copy-start | bytes 12582916
  11.5 2.8 %copy-start.7 = (f32[512]{0:T(512)S(1)}, f32[512]{0:T(512)}, u32[]{:S(2)}) copy-start(f32[512]{0:T(512)} %param.17) | copy-start | bytes 6148
  11.5 2.8 %copy-start.8 = (s32[512]{0:T(512)S(1)}, s32[512]{0:T(512)}, u32[]{:S(2)}) copy-start(s32[512]{0:T(512)} %param.15) | copy-start | bytes 6148
  11.5 3.5 %copy-start.9 = (f32[512]{0:T(512)S(1)}, f32[512]{0:T(512)}, u32[]{:S(2)}) copy-start(f32[512]{0:T(512)} %param.16) | copy-start | bytes 6148
  13.5 25.1 %copy-start.3 = (bf16[512,2048]{1,0:T(8,128)(2,1)}, bf16[512,2048]{1,0:T(8,128)(2,1)S(1)}, u32[]{:S(2)}) copy-start(bf16[512,2048]{1,0:T(8,128)(2,1)S(1)} %get-tuple-element.8) | copy-start | bytes 6291460
  13.5 2.1 %copy-start.5 = (f32[512]{0:T(512)S(1)}, f32[512]{0:T(512)}, u32[]{:S(2)}) copy-start(f32[512]{0:T(512)} %param.13) | copy-start | bytes 6148
  13.5 2.1 %copy-start.6 = (f32[512]{0:T(512)S(1)}, f32[512]{0:T(512)}, u32[]{:S(2)}) copy-start(f32[512]{0:T(512)} %param.14) | copy-start | bytes 6148
